TPU v7x, 512 devices: a whole 4x4x16 slice. The times are simulated.
512 devices in a mesh: gx: 32 (over z, core), gy: 16 (over x, y).
Axes of the slice: x: 4, y: 4, z: 16, core: 2. Of those that a mesh axis runs over, the one named last changes fastest.
Arguments:
- adjoint: float32 [3, 8, 512, 2048], P(None, None, 'gx', 'gy'), may hold values from -12 to 12
- checkpoints: bfloat16 [1, 3, 8, 512, 2048], P(None, None, None, 'gx', 'gy'), may hold values from -3 to 3
- wall_faces: int32 [2, 64, 256], P(None, 'gx', 'gy'), may hold values 0 or 1
Outputs:
- velocity: float32 [3, 8, 512, 2048], P(None, None, 'gx', 'gy')
- pressure: float32 [8, 512, 2048], P(None, 'gx', 'gy')
Inputs may be any that keep to these rules, and one draw needn't show every extreme that they name: `wall_faces`: 1 marks a no-slip face, 0 an open one.
All inputs are finite; a program needn't handle non-finite values. No bound on the sum of `wall_faces` on one device may be relied on, other than what follows from the above.
Results may differ from a plain program's by a relative error of at most 0.0003.
Values sent between devices are 32-bit elements; how exact they have to be, the bound alone decides.
No kernel may reach another device: no remote copies, remote signals or barrier semaphores. Data moves between devices by JAX's collectives and lax.ppermute only.
A program may use at most 64 MiB of HBM per device.

v0:
```python
import jax
import jax.numpy as jnp
import numpy as np
from jax import lax
from jax.sharding import PartitionSpec as P

ITERS = 4
node_points = np.array(
    [
        -1.0,
        -0.8717401485096066,
        -0.5917001814331423,
        -0.2092992179024789,
        0.2092992179024789,
        0.5917001814331423,
        0.8717401485096066,
        1.0,
    ]
)
node_weights = np.array(
    [
        0.03571428571428571,
        0.2107042271435061,
        0.3411226924835044,
        0.4124587946587038,
        0.4124587946587038,
        0.3411226924835044,
        0.2107042271435061,
        0.03571428571428571,
    ]
)
time_step = 0.05
viscosity = 0.02
highest = lax.Precision.HIGHEST


def with_halo(value, sides, width):
    for axis, dim in sides:
        size, length = (lax.axis_size(axis), value.shape[dim])
        up = [(i, (i + 1) % size) for i in range(size)]
        down = [(j, i) for i, j in up]
        last = lax.slice_in_dim(value, length - width, length, axis=dim)
        initial = lax.slice_in_dim(value, 0, width, axis=dim)
        before = lax.ppermute(last, axis, up)
        after = lax.ppermute(initial, axis, down)
        value = jnp.concatenate([before, value, after], axis=dim)
    return value


def derivative_table(points):
    identity = np.eye(points.shape[0])
    spacing = points[:, None] - points[None, :] + identity
    barycentric = 1.0 / np.prod(spacing, axis=1)
    matrix = barycentric[None, :] / barycentric[:, None] / spacing
    matrix = matrix * (1.0 - identity)
    return matrix - identity * np.sum(matrix, axis=1)[:, None]


def along_rows(nodal, matrix):
    blocked = jnp.asarray(np.kron(np.eye(nodal.shape[2] // 8), matrix), jnp.float32)
    return jnp.einsum("xk,czky->czxy", blocked, nodal, precision=highest)


def along_columns(nodal, matrix):
    size_y = nodal.shape[3]
    block_width = 128 if size_y % 128 == 0 else size_y
    blocked = jnp.asarray(np.kron(np.eye(block_width // 8), matrix).T, jnp.float32)
    grouped = nodal.reshape(
        nodal.shape[0], nodal.shape[1], nodal.shape[2], size_y // block_width, block_width
    )
    result = jnp.einsum("czxgk,kb->czxgb", grouped, blocked, precision=highest)
    return result.reshape(nodal.shape)


def along_depth(nodal, matrix):
    return jnp.einsum("ck,akxy->acxy", jnp.asarray(matrix, jnp.float32), nodal, precision=highest)


def mass_weights(size_x, size_y):
    weights = jnp.asarray(node_weights, jnp.float32)
    across_x = jnp.tile(weights, size_x // 8)
    across_y = jnp.tile(weights, size_y // 8)
    return weights[:, None, None] * across_x[None, :, None] * across_y[None, None, :]


def edge_flags(length):
    place = jnp.arange(length) % 8
    return ((place == 0) | (place == 7)).astype(jnp.float32)


def share_counts(size_x, size_y):
    return (1.0 + edge_flags(size_x))[:, None] * (1.0 + edge_flags(size_y))[None, :]


def boundary_masks(wall_faces, size_x, size_y):
    walls = jnp.repeat(jnp.repeat(wall_faces.astype(jnp.float32), 8, axis=1), 8, axis=2)
    interior = (1.0 - edge_flags(size_x))[:, None] * (1.0 - edge_flags(size_y))[None, :]
    middle = jnp.ones((6, size_x, size_y), jnp.float32)
    velocity_mask = jnp.concatenate(
        [(interior * (1.0 - walls[0]))[None], middle, (interior * (1.0 - walls[1]))[None]], axis=0
    )
    pressure_mask = jnp.concatenate(
        [(interior * walls[0])[None], middle, (interior * walls[1])[None]], axis=0
    )
    return (velocity_mask, pressure_mask)


def sum_rows(padded):
    size_x = padded.shape[2] - 2
    place = jnp.arange(size_x) % 8
    upper = (place == 7).astype(jnp.float32)[:, None]
    lower = (place == 0).astype(jnp.float32)[:, None]
    return padded[:, :, 1:-1, :] + upper * padded[:, :, 2:, :] + lower * padded[:, :, :-2, :]


def sum_columns(padded):
    size_y = padded.shape[3] - 2
    place = jnp.arange(size_y) % 8
    upper = (place == 7).astype(jnp.float32)
    lower = (place == 0).astype(jnp.float32)
    return padded[:, :, :, 1:-1] + upper * padded[:, :, :, 2:] + lower * padded[:, :, :, :-2]


def assemble_velocity(nodal):
    padded = with_halo(nodal, (("gx", 2), ("gy", 3)), 1)
    return sum_columns(sum_rows(padded))


def assemble_pressure(nodal):
    padded = with_halo(nodal, (("gx", 2), ("gy", 3)), 1)
    return sum_columns(sum_rows(padded))


def stiffness(nodal, wmass):
    derivative = derivative_table(node_points)
    transposed = derivative.T
    return (
        along_rows(wmass * along_rows(nodal, derivative), transposed)
        + along_columns(wmass * along_columns(nodal, derivative), transposed)
        + along_depth(wmass * along_depth(nodal, derivative), transposed)
    )


def inner(former, latter, inverse_share):
    return jnp.sum(former * latter * inverse_share)


def solve_pressure(source, pressure_mask, wmass, inverse_share):
    pressure = jnp.zeros_like(source)
    resid = source
    direction = source
    norm_now = jnp.zeros((), jnp.float32)
    for round_index in range(ITERS):
        image = pressure_mask * assemble_pressure(stiffness(direction, wmass))
        if round_index == 0:
            norm_now, curve = lax.psum(
                (inner(resid, resid, inverse_share), inner(direction, image, inverse_share)),
                ("gx", "gy"),
            )
        else:
            curve = lax.psum(inner(direction, image, inverse_share), ("gx", "gy"))
        step_length = norm_now / curve
        pressure = pressure + step_length * direction
        resid = resid - step_length * image
        if round_index + 1 < ITERS:
            norm_next = lax.psum(inner(resid, resid, inverse_share), ("gx", "gy"))
            direction = resid + norm_next / norm_now * direction
            norm_now = norm_next
    return pressure


def adjoint_step(velocity, forward, velocity_mask, pressure_mask, wmass, amass, inverse_share):
    derivative = derivative_table(node_points)
    flow = forward.astype(jnp.float32)
    flow_dx = along_rows(flow, derivative)
    flow_dy = along_columns(flow, derivative)
    flow_dz = along_depth(flow, derivative)
    velocity_dx = along_rows(velocity, derivative)
    velocity_dy = along_columns(velocity, derivative)
    velocity_dz = along_depth(velocity, derivative)
    transport = flow[0:1] * velocity_dx + flow[1:2] * velocity_dy + flow[2:3] * velocity_dz
    stretch = jnp.concatenate(
        [
            jnp.sum(velocity * flow_dx, axis=0, keepdims=True),
            jnp.sum(velocity * flow_dy, axis=0, keepdims=True),
            jnp.sum(velocity * flow_dz, axis=0, keepdims=True),
        ],
        axis=0,
    )
    advect = transport - stretch
    forcing = wmass * (velocity + time_step * advect) - time_step * viscosity * stiffness(
        velocity, wmass
    )
    moved = velocity_mask * assemble_velocity(forcing) / amass
    diverge = (
        along_rows(moved[0:1], derivative)
        + along_columns(moved[1:2], derivative)
        + along_depth(moved[2:3], derivative)
    )
    source = -pressure_mask * assemble_pressure(wmass * diverge)
    pressure = solve_pressure(source, pressure_mask, wmass, inverse_share)
    slopes = jnp.concatenate(
        [
            along_rows(pressure, derivative),
            along_columns(pressure, derivative),
            along_depth(pressure, derivative),
        ],
        axis=0,
    )
    correction = assemble_velocity(wmass * slopes) / amass
    return (velocity_mask * (moved - correction), pressure)


def local(adjoint, checkpoints, wall_faces):
    size_x = adjoint.shape[2]
    size_y = adjoint.shape[3]
    wmass = mass_weights(size_x, size_y)
    counts = share_counts(size_x, size_y)
    inverse_share = 1.0 / counts
    amass = wmass * counts
    velocity_mask, pressure_mask = boundary_masks(wall_faces, size_x, size_y)
    velocity = adjoint
    velocity, pressure = adjoint_step(
        velocity, checkpoints[0], velocity_mask, pressure_mask, wmass, amass, inverse_share
    )
    return (velocity, pressure[0])


def solution(mesh):
    return jax.shard_map(
        local,
        mesh=mesh,
        in_specs=(P(None, None, "gx", "gy"), P(None, None, None, "gx", "gy"), P(None, "gx", "gy")),
        out_specs=(P(None, None, "gx", "gy"), P(None, "gx", "gy")),
        check_vma=False,
    )
```

profile of v0, /device:TPU:1, one launch (start us, length us, event | category | flops | bytes accessed | tf_op | source)
XLA Modules:
  0.0 876.8 jit_solution(5244411411854615604)
XLA Ops:
  1.3 1.3 convolution_bitcast_fusion.3
  9.0 3.0 collective-permute-start
  12.1 3.9 collective-permute-start.1
  17.0 1.9 collective-permute-start.2
  18.9 6.7 collective-permute-start.3
  25.6 2.2 collective-permute-done.2
  27.8 1.5 collective-permute-done.3
  32.4 1.8 collective-permute-start.4
  34.3 3.5 collective-permute-start.5
  38.7 1.9 collective-permute-start.6
  40.6 7.4 collective-permute-start.7
  48.1 1.6 collective-permute-done.7
  53.3 6.4 collective-permute-start.9
  60.6 1.9 collective-permute-start.10
  62.6 7.4 collective-permute-start.11
  70.0 1.6 collective-permute-done.11
  72.6 108.5 %all-reduce = (f32[]{:T(128)}, f32[]{:T(128)}) all-reduce(f32[]{:T(128)} %get-tuple-element.3, f32[]{:T(128)} %get-tuple-element.2), channel_id=1, replica_groups=mesh['gx'=32,'gy'=16] {'gx','gy'}, use_global_device_ids=true, to_apply=%region_4.5 | all-reduce | flops 2 | bytes 16 | tf_op jit(solution)/shard_map/psum | solution.py:156
  183.2 98.5 %psum.58 = f32[]{:T(128)} all-reduce(f32[]{:T(128)} %multiply_reduce_fusion.4), channel_id=1, replica_groups=mesh['gx'=32,'gy'=16] {'gx','gy'}, use_global_device_ids=true, to_apply=%region_8.9 | all-reduce | flops 1 | bytes 8 | tf_op jit(solution)/shard_map/psum | solution.py:166
  284.5 2.3 collective-permute-start.12
  287.6 2.3 collective-permute-done.13
  289.9 2.2 collective-permute-start.14
  292.2 6.4 collective-permute-start.15
  298.6 1.4 collective-permute-done.14
  299.9 0.9 collective-permute-done.15
  301.8 102.7 %psum.59 = f32[]{:T(128)} all-reduce(f32[]{:T(128)} %get-tuple-element.10), channel_id=1, replica_groups=mesh['gx'=32,'gy'=16] {'gx','gy'}, use_global_device_ids=true, to_apply=%region_10.11 | all-reduce | flops 1 | bytes 8 | tf_op jit(solution)/shard_map/psum | solution.py:161
  406.6 99.3 %psum.60 = f32[]{:T(128)} all-reduce(f32[]{:T(128)} %get-tuple-element.8), channel_id=1, replica_groups=mesh['gx'=32,'gy'=16] {'gx','gy'}, use_global_device_ids=true, to_apply=%region_12.13 | all-reduce | flops 1 | bytes 8 | tf_op jit(solution)/shard_map/psum | solution.py:166
  508.6 1.4 collective-permute-start.16
  510.8 2.3 collective-permute-done.17
  513.3 2.3 collective-permute-start.18
  515.6 6.3 collective-permute-start.19
  522.4 1.1 collective-permute-done.19
  524.5 104.3 %psum.61 = f32[]{:T(128)} all-reduce(f32[]{:T(128)} %get-tuple-element.6), channel_id=1, replica_groups=mesh['gx'=32,'gy'=16] {'gx','gy'}, use_global_device_ids=true, to_apply=%region_14.15 | all-reduce | flops 1 | bytes 8 | tf_op jit(solution)/shard_map/psum | solution.py:161
  630.8 98.4 %psum.62 = f32[]{:T(128)} all-reduce(f32[]{:T(128)} %multiply_reduce_fusion), channel_id=1, replica_groups=mesh['gx'=32,'gy'=16] {'gx','gy'}, use_global_device_ids=true, to_apply=%region_16.17 | all-reduce | flops 1 | bytes 8 | tf_op jit(solution)/shard_map/psum | solution.py:166
  731.9 2.3 collective-permute-start.20
  735.0 2.3 collective-permute-done.21
  737.4 2.5 collective-permute-start.22
  739.9 6.1 collective-permute-start.23
  746.0 1.4 collective-permute-done.22
  747.4 0.9 collective-permute-done.23
  749.3 102.6 %psum.63 = f32[]{:T(128)} all-reduce(f32[]{:T(128)} %fusion.73), channel_id=1, replica_groups=mesh['gx'=32,'gy'=16] {'gx','gy'}, use_global_device_ids=true, to_apply=%region_18.19 | all-reduce | flops 1 | bytes 8 | tf_op jit(solution)/shard_map/psum | solution.py:161
  854.3 2.7 collective-permute-start.24
  857.0 0.8 collective-permute-done.24
  857.8 2.3 collective-permute-done.25
  860.3 1.9 collective-permute-start.26
  862.2 6.7 collective-permute-start.27
  868.9 5.4 collective-permute-done.26
  874.3 1.0 collective-permute-done.27
  875.8 1.0 fusion.35
  (175 shorter events, 31.4 us)
Async XLA Ops:
  0.6 0.7 copy-start.11
  1.3 1.3 copy-start
  1.3 1.3 copy-start.2
  2.7 0.8 copy-start.6
  4.1 0.7 copy-start.15
  4.9 0.7 copy-start.12
  6.4 0.7 copy-start.13
  7.1 0.7 copy-start.14
  7.7 0.8 copy-start.10
  9.0 7.6 collective-permute-start
  12.1 3.9 copy-start.16
  12.1 4.7 collective-permute-start.1
  17.0 10.8 %collective-permute-start.2 = (f32[3,8,18,1]{3,2,1,0:T(8,128)S(1)}, f32[3,8,18,1]{3,2,1,0:T(8,128)S(1)}, u32[]{:S(2)}, u32[]{:S(2)}) collective-permute-start(f32[3,8,18,1]{3,2,1,0:T(8,128)S(1)} %get-tuple-element.15), channel_id=1, source_target_pairs={{0,1},{1,2},{2,3},{3,4},{4,5},{5,6},{6,7},{7,8},{8,9},{9,10},{10,1... | collective-permute-start | bytes 5192 | tf_op jit(solution)/shard_map/ppermute | solution.py:44
  18.9 10.3 %collective-permute-start.3 = (f32[3,8,18,1]{3,2,1,0:T(8,128)S(1)}, f32[3,8,18,1]{3,2,1,0:T(8,128)S(1)}, u32[]{:S(2)}, u32[]{:S(2)}) collective-permute-start(f32[3,8,18,1]{3,2,1,0:T(8,128)S(1)} %get-tuple-element.16), channel_id=1, source_target_pairs={{1,0},{2,1},{3,2},{4,3},{5,4},{6,5},{7,6},{8,7},{9,8},{10,9},{11,1... | collective-permute-start | bytes 5192 | tf_op jit(solution)/shard_map/ppermute | solution.py:45
  30.0 0.8 copy-start.1
  30.8 0.7 copy-start.7
  31.5 0.7 copy-start.5
  32.4 5.9 collective-permute-start.4
  34.3 4.3 collective-permute-start.5
  38.7 9.4 %collective-permute-start.6 = (f32[1,8,18,1]{3,2,1,0:T(8,128)S(1)}, f32[1,8,18,1]{3,2,1,0:T(8,128)S(1)}, u32[]{:S(2)}, u32[]{:S(2)}) collective-permute-start(f32[1,8,18,1]{3,2,1,0:T(8,128)S(1)} %get-tuple-element.32), channel_id=1, source_target_pairs={{0,1},{1,2},{2,3},{3,4},{4,5},{5,6},{6,7},{7,8},{8,9},{9,10},{10,1... | collective-permute-start | bytes 1736 | tf_op jit(solution)/shard_map/ppermute | solution.py:44
  40.6 9.1 %collective-permute-start.7 = (f32[1,8,18,1]{3,2,1,0:T(8,128)S(1)}, f32[1,8,18,1]{3,2,1,0:T(8,128)S(1)}, u32[]{:S(2)}, u32[]{:S(2)}) collective-permute-start(f32[1,8,18,1]{3,2,1,0:T(8,128)S(1)} %get-tuple-element.33), channel_id=1, source_target_pairs={{1,0},{2,1},{3,2},{4,3},{5,4},{6,5},{7,6},{8,7},{9,8},{10,9},{11,1... | collective-permute-start | bytes 1736 | tf_op jit(solution)/shard_map/ppermute | solution.py:45
  50.8 0.8 copy-start.3
  51.6 0.7 copy-start.9
  52.3 0.7 copy-start.8
  53.3 7.1 collective-permute-start.8
  53.3 7.3 collective-permute-start.9
  60.6 9.4 %collective-permute-start.10 = (f32[1,8,18,1]{3,2,1,0:T(8,128)S(1)}, f32[1,8,18,1]{3,2,1,0:T(8,128)S(1)}, u32[]{:S(2)}, u32[]{:S(2)}) collective-permute-start(f32[1,8,18,1]{3,2,1,0:T(8,128)S(1)} %get-tuple-element.30), channel_id=1, source_target_pairs={{0,1},{1,2},{2,3},{3,4},{4,5},{5,6},{6,7},{7,8},{8,9},{9,10},{10,1... | collective-permute-start | bytes 1736 | tf_op jit(solution)/shard_map/ppermute | solution.py:44
  62.6 9.0 %collective-permute-start.11 = (f32[1,8,18,1]{3,2,1,0:T(8,128)S(1)}, f32[1,8,18,1]{3,2,1,0:T(8,128)S(1)}, u32[]{:S(2)}, u32[]{:S(2)}) collective-permute-start(f32[1,8,18,1]{3,2,1,0:T(8,128)S(1)} %get-tuple-element.31), channel_id=1, source_target_pairs={{1,0},{2,1},{3,2},{4,3},{5,4},{6,5},{7,6},{8,7},{9,8},{10,9},{11,1... | collective-permute-start | bytes 1736 | tf_op jit(solution)/shard_map/ppermute | solution.py:45
  284.5 3.1 collective-permute-start.12
  286.8 3.0 collective-permute-start.13
  289.9 10.0 %collective-permute-start.14 = (f32[1,8,18,1]{3,2,1,0:T(8,128)S(1)}, f32[1,8,18,1]{3,2,1,0:T(8,128)S(1)}, u32[]{:S(2)}, u32[]{:S(2)}) collective-permute-start(f32[1,8,18,1]{3,2,1,0:T(8,128)S(1)} %get-tuple-element.28), channel_id=1, source_target_pairs={{0,1},{1,2},{2,3},{3,4},{4,5},{5,6},{6,7},{7,8},{8,9},{9,10},{10,1... | collective-permute-start | bytes 1736 | tf_op jit(solution)/shard_map/ppermute | solution.py:44
  292.2 8.7 collective-permute-start.15
  508.6 2.2 collective-permute-start.16
  510.1 3.1 collective-permute-start.17
  513.3 9.1 %collective-permute-start.18 = (f32[1,8,18,1]{3,2,1,0:T(8,128)S(1)}, f32[1,8,18,1]{3,2,1,0:T(8,128)S(1)}, u32[]{:S(2)}, u32[]{:S(2)}) collective-permute-start(f32[1,8,18,1]{3,2,1,0:T(8,128)S(1)} %get-tuple-element.26), channel_id=1, source_target_pairs={{0,1},{1,2},{2,3},{3,4},{4,5},{5,6},{6,7},{7,8},{8,9},{9,10},{10,1... | collective-permute-start | bytes 1736 | tf_op jit(solution)/shard_map/ppermute | solution.py:44
  515.6 7.9 collective-permute-start.19
  731.9 3.1 collective-permute-start.20
  734.3 3.0 collective-permute-start.21
  737.4 10.0 %collective-permute-start.22 = (f32[1,8,18,1]{3,2,1,0:T(8,128)S(1)}, f32[1,8,18,1]{3,2,1,0:T(8,128)S(1)}, u32[]{:S(2)}, u32[]{:S(2)}) collective-permute-start(f32[1,8,18,1]{3,2,1,0:T(8,128)S(1)} %get-tuple-element.24), channel_id=1, source_target_pairs={{0,1},{1,2},{2,3},{3,4},{4,5},{5,6},{6,7},{7,8},{8,9},{9,10},{10,1... | collective-permute-start | bytes 1736 | tf_op jit(solution)/shard_map/ppermute | solution.py:44
  739.9 8.4 collective-permute-start.23
  853.4 0.6 copy-start.4
  854.3 3.5 collective-permute-start.24
  857.0 3.1 collective-permute-start.25
  860.3 14.0 %collective-permute-start.26 = (f32[3,8,18,1]{3,2,1,0:T(8,128)S(1)}, f32[3,8,18,1]{3,2,1,0:T(8,128)S(1)}, u32[]{:S(2)}, u32[]{:S(2)}) collective-permute-start(f32[3,8,18,1]{3,2,1,0:T(8,128)S(1)} %get-tuple-element.13), channel_id=1, source_target_pairs={{0,1},{1,2},{2,3},{3,4},{4,5},{5,6},{6,7},{7,8},{8,9},{9,10},{10,1... | collective-permute-start | bytes 5192 | tf_op jit(solution)/shard_map/ppermute | solution.py:44
  862.2 13.1 %collective-permute-start.27 = (f32[3,8,18,1]{3,2,1,0:T(8,128)S(1)}, f32[3,8,18,1]{3,2,1,0:T(8,128)S(1)}, u32[]{:S(2)}, u32[]{:S(2)}) collective-permute-start(f32[3,8,18,1]{3,2,1,0:T(8,128)S(1)} %get-tuple-element.14), channel_id=1, source_target_pairs={{1,0},{2,1},{3,2},{4,3},{5,4},{6,5},{7,6},{8,7},{9,8},{10,9},{11,1... | collective-permute-start | bytes 5192 | tf_op jit(solution)/shard_map/ppermute | solution.py:45
where the time goes:
time: 879 us; the launch traced here: 877 us
  blocking collectives  714 us (81%)
  starting transfers between devices  89.1 us (10%)
  waiting for transfers between devices  33.5 us (4%)
  between operations  10.9 us (1%)
  other arithmetic  10 us (1%)
  matrix products  9.55 us (1%)
  local copies, waits for them, and re-layouts  9.23 us (1%)
    psum x3, blocking collectives, solve_pressure(): curve = lax.psum(inner(direction, image, inverse_share), ('gx', 'gy'))  310 us
    psum x3, blocking collectives, solve_pressure(): norm_next = lax.psum(inner(resid, resid, inverse_share), ('gx', 'gy'))  296 us
    psum x1, blocking collectives, solve_pressure(): lax.psum((inner(resid, resid, inverse_share), inner(direction, image, inv...  109 us
    ppermute x14, starting transfers between devices, with_halo(): after = lax.ppermute(initial, axis, down)  60.8 us
    ppermute x14, starting transfers between devices, with_halo(): before = lax.ppermute(last, axis, up)  28.4 us
    ppermute x14, waiting for transfers between devices, with_halo(): after = lax.ppermute(initial, axis, down)  18.2 us
  transfers between devices with their start and end apart: 28, of which 27 were waited for; matrix products, arithmetic and copies ran while one was open for 0% of the time, Pallas kernels for 0%

commit v1 on v0

--- a/solution.py
+++ b/solution.py
@@ -34,6 +34,11 @@
 highest = lax.Precision.HIGHEST
 
 
+def axis_by_axis(array, inner_axis, outer_axis):
+    half = lax.psum(array, inner_axis)
+    return lax.psum(half, outer_axis)
+
+
 def with_halo(value, sides, width):
     for axis, dim in sides:
         size, length = (lax.axis_size(axis), value.shape[dim])
@@ -163,7 +168,7 @@
         pressure = pressure + step_length * direction
         resid = resid - step_length * image
         if round_index + 1 < ITERS:
-            norm_next = lax.psum(inner(resid, resid, inverse_share), ("gx", "gy"))
+            norm_next = axis_by_axis(inner(resid, resid, inverse_share), "gy", "gx")
             direction = resid + norm_next / norm_now * direction
             norm_now = norm_next
     return pressure

time: 879 us -> 832 us (0.947)
  blocking collectives: 714 us -> 677 us
    psum x3 -> x6, blocking collectives: 296 us -> 252 us  [the longest x3 161 us: axis_by_axis(): return lax.psum(half, outer_axis)]
where the time goes in v1:
time: 832 us; the launch traced here: 828 us
  blocking collectives  677 us (81%)
  starting transfers between devices  83.6 us (10%)
  waiting for transfers between devices  26.8 us (3%)
  between operations  11 us (1%)
  other arithmetic  10 us (1%)
  matrix products  9.55 us (1%)
  local copies, waits for them, and re-layouts  9.23 us (1%)
    psum x3, blocking collectives, solve_pressure(): curve = lax.psum(inner(direction, image, inverse_share), ('gx', 'gy'))  317 us
    psum x3, blocking collectives, axis_by_axis(): return lax.psum(half, outer_axis)  161 us
    psum x1, blocking collectives, solve_pressure(): lax.psum((inner(resid, resid, inverse_share), inner(direction, image, inv...  109 us
    psum x3, blocking collectives, axis_by_axis(): half = lax.psum(array, inner_axis)  90.8 us
    ppermute x14, starting transfers between devices, with_halo(): after = lax.ppermute(initial, axis, down)  62.5 us
    ppermute x14, starting transfers between devices, with_halo(): before = lax.ppermute(last, axis, up)  21.1 us
    ppermute x14, waiting for transfers between devices, with_halo(): after = lax.ppermute(initial, axis, down)  17.5 us
  transfers between devices with their start and end apart: 28, of which 27 were waited for; matrix products, arithmetic and copies ran while one was open for 0% of the time, Pallas kernels for 0%

profile of v1, /device:TPU:1, one launch (start us, length us, event | category | flops | bytes accessed | tf_op | source)
XLA Modules:
  0.0 827.5 jit_solution(11909358740170455451)
XLA Ops:
  1.3 1.3 convolution_bitcast_fusion.3
  9.0 3.0 collective-permute-start
  12.1 3.9 collective-permute-start.1
  17.0 1.9 collective-permute-start.2
  18.9 6.7 collective-permute-start.3
  25.6 2.2 collective-permute-done.2
  27.8 1.5 collective-permute-done.3
  30.0 0.8 copy-done.1
  32.4 1.8 collective-permute-start.4
  34.3 3.5 collective-permute-start.5
  38.7 1.9 collective-permute-start.6
  40.6 7.4 collective-permute-start.7
  48.1 1.6 collective-permute-done.7
  50.9 0.7 copy-done.3
  53.3 6.4 collective-permute-start.9
  60.6 1.9 collective-permute-start.10
  62.6 7.4 collective-permute-start.11
  70.0 1.6 collective-permute-done.11
  71.8 0.8 multiply_reduce_fusion.5
  72.6 108.5 %all-reduce = (f32[]{:T(128)}, f32[]{:T(128)}) all-reduce(f32[]{:T(128)} %get-tuple-element.3, f32[]{:T(128)} %get-tuple-element.2), channel_id=1, replica_groups=mesh['gx'=32,'gy'=16] {'gx','gy'}, use_global_device_ids=true, to_apply=%region_4.5 | all-reduce | flops 2 | bytes 16 | tf_op jit(solution)/shard_map/psum | solution.py:161
  183.2 30.3 %psum.79 = f32[]{:T(128)} all-reduce(f32[]{:T(128)} %multiply_reduce_fusion.4), channel_id=1, replica_groups=mesh['gx'=32,'gy'=16] {'gy'}, use_global_device_ids=true, to_apply=%region_8.9 | all-reduce | flops 1 | bytes 8 | tf_op jit(solution)/shard_map/psum | solution.py:38
  213.5 53.7 %psum.80 = f32[]{:T(128)} all-reduce(f32[]{:T(128)} %psum.79), channel_id=1, replica_groups=mesh['gx'=32,'gy'=16] {'gx'}, use_global_device_ids=true, to_apply=%region_9.10 | all-reduce | flops 1 | bytes 8 | tf_op jit(solution)/shard_map/psum | solution.py:39
  271.3 1.8 collective-permute-done.13
  273.2 2.5 collective-permute-start.14
  275.7 6.1 collective-permute-start.15
  281.8 1.6 collective-permute-done.15
  284.4 105.6 %psum.81 = f32[]{:T(128)} all-reduce(f32[]{:T(128)} %get-tuple-element.10), channel_id=1, replica_groups=mesh['gx'=32,'gy'=16] {'gx','gy'}, use_global_device_ids=true, to_apply=%region_11.12 | all-reduce | flops 1 | bytes 8 | tf_op jit(solution)/shard_map/psum | solution.py:166
  392.0 30.3 %psum.82 = f32[]{:T(128)} all-reduce(f32[]{:T(128)} %get-tuple-element.8), channel_id=1, replica_groups=mesh['gx'=32,'gy'=16] {'gy'}, use_global_device_ids=true, to_apply=%region_13.14 | all-reduce | flops 1 | bytes 8 | tf_op jit(solution)/shard_map/psum | solution.py:38
  422.3 53.7 %psum.83 = f32[]{:T(128)} all-reduce(f32[]{:T(128)} %psum.82), channel_id=1, replica_groups=mesh['gx'=32,'gy'=16] {'gx'}, use_global_device_ids=true, to_apply=%region_14.15 | all-reduce | flops 1 | bytes 8 | tf_op jit(solution)/shard_map/psum | solution.py:39
  480.0 1.7 collective-permute-done.17
  481.9 2.7 collective-permute-start.18
  484.6 5.9 collective-permute-start.19
  490.6 1.6 collective-permute-done.19
  493.1 105.6 %psum.84 = f32[]{:T(128)} all-reduce(f32[]{:T(128)} %get-tuple-element.6), channel_id=1, replica_groups=mesh['gx'=32,'gy'=16] {'gx','gy'}, use_global_device_ids=true, to_apply=%region_16.17 | all-reduce | flops 1 | bytes 8 | tf_op jit(solution)/shard_map/psum | solution.py:166
  600.7 30.3 %psum.85 = f32[]{:T(128)} all-reduce(f32[]{:T(128)} %multiply_reduce_fusion), channel_id=1, replica_groups=mesh['gx'=32,'gy'=16] {'gy'}, use_global_device_ids=true, to_apply=%region_18.19 | all-reduce | flops 1 | bytes 8 | tf_op jit(solution)/shard_map/psum | solution.py:38
  630.9 53.9 %psum.86 = f32[]{:T(128)} all-reduce(f32[]{:T(128)} %psum.85), channel_id=1, replica_groups=mesh['gx'=32,'gy'=16] {'gx'}, use_global_device_ids=true, to_apply=%region_19.20 | all-reduce | flops 1 | bytes 8 | tf_op jit(solution)/shard_map/psum | solution.py:39
  688.9 1.7 collective-permute-done.21
  690.7 2.7 collective-permute-start.22
  693.4 5.9 collective-permute-start.23
  699.4 1.6 collective-permute-done.23
  701.9 105.6 %psum.87 = f32[]{:T(128)} all-reduce(f32[]{:T(128)} %fusion.73), channel_id=1, replica_groups=mesh['gx'=32,'gy'=16] {'gx','gy'}, use_global_device_ids=true, to_apply=%region_21.22 | all-reduce | flops 1 | bytes 8 | tf_op jit(solution)/shard_map/psum | solution.py:166
  810.2 0.9 collective-permute-start.25
  811.8 1.5 collective-permute-done.25
  813.5 2.1 collective-permute-start.26
  815.7 6.5 collective-permute-start.27
  822.1 3.0 collective-permute-done.26
  825.1 0.9 collective-permute-done.27
  826.6 1.0 fusion.35
  (178 shorter events, 31.3 us)
Async XLA Ops:
  0.6 0.7 copy-start.11
  1.3 1.3 copy-start
  1.3 1.3 copy-start.2
  2.7 0.8 copy-start.6
  4.1 0.7 copy-start.15
  4.9 0.7 copy-start.12
  6.4 0.7 copy-start.13
  7.1 0.7 copy-start.14
  7.7 0.8 copy-start.10
  9.0 7.6 collective-permute-start
  12.1 3.9 copy-start.16
  12.1 4.7 collective-permute-start.1
  17.0 10.8 %collective-permute-start.2 = (f32[3,8,18,1]{3,2,1,0:T(8,128)S(1)}, f32[3,8,18,1]{3,2,1,0:T(8,128)S(1)}, u32[]{:S(2)}, u32[]{:S(2)}) collective-permute-start(f32[3,8,18,1]{3,2,1,0:T(8,128)S(1)} %get-tuple-element.15), channel_id=1, source_target_pairs={{0,1},{1,2},{2,3},{3,4},{4,5},{5,6},{6,7},{7,8},{8,9},{9,10},{10,1... | collective-permute-start | bytes 5192 | tf_op jit(solution)/shard_map/ppermute | solution.py:49
  18.9 10.3 %collective-permute-start.3 = (f32[3,8,18,1]{3,2,1,0:T(8,128)S(1)}, f32[3,8,18,1]{3,2,1,0:T(8,128)S(1)}, u32[]{:S(2)}, u32[]{:S(2)}) collective-permute-start(f32[3,8,18,1]{3,2,1,0:T(8,128)S(1)} %get-tuple-element.16), channel_id=1, source_target_pairs={{1,0},{2,1},{3,2},{4,3},{5,4},{6,5},{7,6},{8,7},{9,8},{10,9},{11,1... | collective-permute-start | bytes 5192 | tf_op jit(solution)/shard_map/ppermute | solution.py:50
  30.0 0.8 copy-start.1
  30.8 0.7 copy-start.7
  31.5 0.7 copy-start.5
  32.4 5.9 collective-permute-start.4
  34.3 4.3 collective-permute-start.5
  38.7 9.4 %collective-permute-start.6 = (f32[1,8,18,1]{3,2,1,0:T(8,128)S(1)}, f32[1,8,18,1]{3,2,1,0:T(8,128)S(1)}, u32[]{:S(2)}, u32[]{:S(2)}) collective-permute-start(f32[1,8,18,1]{3,2,1,0:T(8,128)S(1)} %get-tuple-element.32), channel_id=1, source_target_pairs={{0,1},{1,2},{2,3},{3,4},{4,5},{5,6},{6,7},{7,8},{8,9},{9,10},{10,1... | collective-permute-start | bytes 1736 | tf_op jit(solution)/shard_map/ppermute | solution.py:49
  40.6 9.1 %collective-permute-start.7 = (f32[1,8,18,1]{3,2,1,0:T(8,128)S(1)}, f32[1,8,18,1]{3,2,1,0:T(8,128)S(1)}, u32[]{:S(2)}, u32[]{:S(2)}) collective-permute-start(f32[1,8,18,1]{3,2,1,0:T(8,128)S(1)} %get-tuple-element.33), channel_id=1, source_target_pairs={{1,0},{2,1},{3,2},{4,3},{5,4},{6,5},{7,6},{8,7},{9,8},{10,9},{11,1... | collective-permute-start | bytes 1736 | tf_op jit(solution)/shard_map/ppermute | solution.py:50
  50.8 0.8 copy-start.3
  51.6 0.7 copy-start.9
  52.3 0.7 copy-start.8
  53.3 7.1 collective-permute-start.8
  53.3 7.3 collective-permute-start.9
  60.6 9.4 %collective-permute-start.10 = (f32[1,8,18,1]{3,2,1,0:T(8,128)S(1)}, f32[1,8,18,1]{3,2,1,0:T(8,128)S(1)}, u32[]{:S(2)}, u32[]{:S(2)}) collective-permute-start(f32[1,8,18,1]{3,2,1,0:T(8,128)S(1)} %get-tuple-element.30), channel_id=1, source_target_pairs={{0,1},{1,2},{2,3},{3,4},{4,5},{5,6},{6,7},{7,8},{8,9},{9,10},{10,1... | collective-permute-start | bytes 1736 | tf_op jit(solution)/shard_map/ppermute | solution.py:49
  62.6 9.0 %collective-permute-start.11 = (f32[1,8,18,1]{3,2,1,0:T(8,128)S(1)}, f32[1,8,18,1]{3,2,1,0:T(8,128)S(1)}, u32[]{:S(2)}, u32[]{:S(2)}) collective-permute-start(f32[1,8,18,1]{3,2,1,0:T(8,128)S(1)} %get-tuple-element.31), channel_id=1, source_target_pairs={{1,0},{2,1},{3,2},{4,3},{5,4},{6,5},{7,6},{8,7},{9,8},{10,9},{11,1... | collective-permute-start | bytes 1736 | tf_op jit(solution)/shard_map/ppermute | solution.py:50
  270.0 1.3 collective-permute-start.12
  270.0 3.0 collective-permute-start.13
  273.2 8.7 %collective-permute-start.14 = (f32[1,8,18,1]{3,2,1,0:T(8,128)S(1)}, f32[1,8,18,1]{3,2,1,0:T(8,128)S(1)}, u32[]{:S(2)}, u32[]{:S(2)}) collective-permute-start(f32[1,8,18,1]{3,2,1,0:T(8,128)S(1)} %get-tuple-element.28), channel_id=1, source_target_pairs={{0,1},{1,2},{2,3},{3,4},{4,5},{5,6},{6,7},{7,8},{8,9},{9,10},{10,1... | collective-permute-start | bytes 1736 | tf_op jit(solution)/shard_map/ppermute | solution.py:49
  275.7 7.7 collective-permute-start.15
  478.7 1.3 collective-permute-start.16
  478.7 3.0 collective-permute-start.17
  481.9 8.7 %collective-permute-start.18 = (f32[1,8,18,1]{3,2,1,0:T(8,128)S(1)}, f32[1,8,18,1]{3,2,1,0:T(8,128)S(1)}, u32[]{:S(2)}, u32[]{:S(2)}) collective-permute-start(f32[1,8,18,1]{3,2,1,0:T(8,128)S(1)} %get-tuple-element.26), channel_id=1, source_target_pairs={{0,1},{1,2},{2,3},{3,4},{4,5},{5,6},{6,7},{7,8},{8,9},{9,10},{10,1... | collective-permute-start | bytes 1736 | tf_op jit(solution)/shard_map/ppermute | solution.py:49
  484.6 7.5 collective-permute-start.19
  687.5 1.3 collective-permute-start.20
  687.6 3.0 collective-permute-start.21
  690.7 8.7 %collective-permute-start.22 = (f32[1,8,18,1]{3,2,1,0:T(8,128)S(1)}, f32[1,8,18,1]{3,2,1,0:T(8,128)S(1)}, u32[]{:S(2)}, u32[]{:S(2)}) collective-permute-start(f32[1,8,18,1]{3,2,1,0:T(8,128)S(1)} %get-tuple-element.24), channel_id=1, source_target_pairs={{0,1},{1,2},{2,3},{3,4},{4,5},{5,6},{6,7},{7,8},{8,9},{9,10},{10,1... | collective-permute-start | bytes 1736 | tf_op jit(solution)/shard_map/ppermute | solution.py:49
  693.4 7.5 collective-permute-start.23
  809.0 0.6 copy-start.4
  809.9 1.9 collective-permute-start.24
  810.2 3.1 collective-permute-start.25
  813.5 11.6 %collective-permute-start.26 = (f32[3,8,18,1]{3,2,1,0:T(8,128)S(1)}, f32[3,8,18,1]{3,2,1,0:T(8,128)S(1)}, u32[]{:S(2)}, u32[]{:S(2)}) collective-permute-start(f32[3,8,18,1]{3,2,1,0:T(8,128)S(1)} %get-tuple-element.13), channel_id=1, source_target_pairs={{0,1},{1,2},{2,3},{3,4},{4,5},{5,6},{6,7},{7,8},{8,9},{9,10},{10,1... | collective-permute-start | bytes 5192 | tf_op jit(solution)/shard_map/ppermute | solution.py:49
  815.7 10.4 %collective-permute-start.27 = (f32[3,8,18,1]{3,2,1,0:T(8,128)S(1)}, f32[3,8,18,1]{3,2,1,0:T(8,128)S(1)}, u32[]{:S(2)}, u32[]{:S(2)}) collective-permute-start(f32[3,8,18,1]{3,2,1,0:T(8,128)S(1)} %get-tuple-element.14), channel_id=1, source_target_pairs={{1,0},{2,1},{3,2},{4,3},{5,4},{6,5},{7,6},{8,7},{9,8},{10,9},{11,1... | collective-permute-start | bytes 5192 | tf_op jit(solution)/shard_map/ppermute | solution.py:50
